TPU v7x, 512 devices: a whole 4x4x16 slice. The times are simulated.
512 devices in a mesh: grp: 64 (over x_lo, z, core), head: 8 (over y, x_hi).
Axes of the slice: x: 4 (x_hi: 2, x_lo: 2; x = x_hi * 2 + x_lo), y: 4, z: 16, core: 2. Of those that a mesh axis runs over, the one named last changes fastest.
Arguments:
- resident_latent_cache: bfloat16 [256, 256, 576], P('grp'), may hold values from -6 to 6
- resident_len: int32 [64, 4], P('grp'), may hold values from 1 to 256, 640 in all within a row
- resident_query: bfloat16 [3, 256, 128, 576], P(None, 'grp', 'head'), may hold values from -49 to 49
- step_latent: bfloat16 [3, 256, 576], P(None, 'grp'), may hold values from -6 to 6
- prompt_cache: bfloat16 [256, 1024, 576], P('grp', 'head'), may hold values from -6 to 6
- prompt_query: bfloat16 [256, 128, 576], P('grp', 'head'), may hold values from -49 to 49
- prompt_len: int32 [64, 4], replicated, may hold values from 1 to 1024, 2560 in all within a row
- route_offset: int32 [64, 4, 1], replicated, may hold values from 0 to 3; in each aligned block of 4 rows (0 to 3, 4 to 7, ..., all dimensions but the last counted through in order) at most 2 rows name the same one
Outputs:
- resident_out: bfloat16 [3, 256, 128, 512], P(None, 'grp', 'head')
- first_out: bfloat16 [64, 8, 128, 512], P('grp', None, 'head')
- arrived_cache: bfloat16 [64, 8, 1024, 576], P('grp', None, 'head')
Inputs may be any that keep to these rules, and one draw needn't show every extreme that they name: `resident_len`: in every group one sequence fills all 256 cache slots. `prompt_len`: in every prefill group one prompt fills all 1024 positions. `route_offset`: among the 4 prompts of one prefill group no value is named more than 2 times; in some prefill groups one value is named exactly 2 times, and every value is named by some prompt.
All inputs are finite; a program needn't handle non-finite values.
Results may differ from a plain program's by a relative error of at most 0.015.
Values may be sent and summed in bfloat16 or wider, within the bound.
A program may use at most 64 MiB of HBM per device.

v0:
```python
import functools

import jax
import jax.numpy as jnp
from jax import lax
from jax.experimental import pallas as pl
from jax.experimental.pallas import tpu as pltpu
from jax.sharding import PartitionSpec as P

LATENT_RANK = 512
REACH = 4
CAPACITY = 2
MESH = pl.DeviceIdType.MESH
SCALE = 192.0 ** (-0.5)
LOW = -1e30
NEW_ROWS = 16

FAR = 2
HALVES = 2
PIECES = 4

NN = (((1,), (0,)), ((), ()))
NT = (((1,), (1,)), ((), ()))


def matmul(a, b, dims):
    return lax.dot_general(a, b, dims, preferred_element_type=jnp.float32)


def kernel(
    groups, lanes,
    plen_hbm, roff_hbm, rlen_hbm, sl, rct, rq, pct, pq,
    ro, fo, ac,
    plen, roff, rlen,
    rctv, rqv, pctv, slv, qall, newk, newkf, obuf, rbuf, stat, rstat, xbuf, xrec, xstat, xrstat, mbuf, mstat, hop, hopstat, given, via, near, picked, frows, fsend, rov,
    load_sem, out_sem, q_send, q_recv, o_send, o_recv, s_send, s_recv, x_send, x_recv, h_send, h_recv,
    w_send, w_recv, n_send, n_recv, p_send, p_recv, keep_sem, f_send, f_recv, v_send, v_recv, b_send,
    *wholes,
):
    me = lax.axis_index("grp")
    lane = lax.axis_index("head")
    core = lax.rem(me, 2)
    prompts, width, part = pct.shape
    seqs = rct.shape[0]
    res_len = rct.shape[2]
    steps, _, heads, _ = rq.shape
    line = lanes // FAR
    piece = width // PIECES

    y, x = lane // FAR, lax.rem(lane, FAR)

    def on_lane(j, k):
        return (me, lax.rem(y + k, line) * FAR + lax.rem(x + j, FAR))

    def on_group(k):
        return (lax.rem(me + k + groups, groups), lane)

    direct = [(1, 0)] + [(0, k) for k in range(1, line)]
    others = direct + [(1, k) for k in range(1, line)]
    turn = lax.rem(me, groups // 2)
    first = turn < 2
    second = jnp.logical_and(turn >= 2, turn < 4)
    mid = (groups // 2 - 4) // 4 * 2
    giver, bearer, taker = turn == groups // 2 - 4, turn == mid, turn == 0
    spared = turn == groups // 2 - 2

    barrier = pltpu.get_barrier_semaphore()

    def greet(to):
        pl.semaphore_signal(barrier, inc=1, device_id=to, device_id_type=MESH)

    def beside(k):
        return (on_group(k)[0], on_lane(1, 0)[1])

    for k in range(REACH, 0, -1):
        greet(on_group(-k))
    for j, k in direct:
        greet(on_lane(j, k))
    pl.when(core == 0)(lambda: greet(on_group(1)))
    pl.when(taker)(lambda: greet(on_group(mid)))
    pl.when(bearer)(lambda: greet(on_group(-mid - 4)))
    pl.when(first)(lambda: greet(on_group(2)))
    pl.when(second)(lambda: greet(beside(-2)))

    loads = [
        pltpu.make_async_copy(src, dst, load_sem.at[i])
        for i, (src, dst) in enumerate(((pct, pctv), (pq, qall.at[0]), (rct, rctv), (rq, rqv), (sl, slv),
                                    (plen_hbm, plen), (roff_hbm, roff), (rlen_hbm, rlen)))
    ]
    for copy in loads:
        copy.start()

    extra = core + jnp.where(jnp.logical_or(first, second), 1, 0)
    extra = extra + jnp.where(jnp.logical_or(giver, bearer), 1, 0)
    pl.semaphore_wait(barrier, len(direct) + REACH + extra)

    def remote(src, dst, send, recv, to):
        return pltpu.make_async_remote_copy(
            src_ref=src, dst_ref=dst, send_sem=send, recv_sem=recv, device_id=to, device_id_type=MESH
        )

    half = prompts // HALVES

    def query_copy(j, k, h):
        slot, held = j * line + k, pl.ds(h * half, half)
        source = qall.at[j * line, held] if j and k else pq.at[held]
        return remote(source, qall.at[slot, held], q_send.at[slot, h], q_recv.at[slot, h], on_lane(0 if k else j, k))

    q_copies = {(j, k, h): query_copy(j, k, h) for j, k in others for h in range(HALVES)}
    for h in range(HALVES):
        q_copies[1, 0, h].start()
    for h in range(HALVES):
        for k in range(1, line):
            q_copies[0, k, h].start()

    def latent(i):
        return pl.ds(i * piece, piece)

    w_copies = [
        remote(pct.at[:, latent(i)], wholes[i], w_send.at[i], w_recv.at[i], on_group(2))
        for i in range(PIECES)
    ]
    for copy in w_copies:
        copy.start()

    def places_of(group):
        offs = [roff[i, group] for i in range(prompts)]
        lens = [plen[i, group] - lane * part for i in range(prompts)]
        ranks = []
        for i in range(prompts):
            rank = jnp.int32(0)
            for i2 in range(i):
                rank = rank + jnp.where(offs[i2] == offs[i], 1, 0)
            ranks.append(rank)

        def pick(distance, place):
            index, length, filled = jnp.int32(0), jnp.int32(0), jnp.int32(0)
            for i in range(prompts):
                hit = jnp.logical_and(offs[i] == distance, ranks[i] == place)
                index = jnp.where(hit, i, index)
                length = jnp.where(hit, lens[i], length)
                filled = jnp.where(hit, 1, filled)
            return index, length, filled

        return lens, [[pick(d, r) for r in range(CAPACITY)] for d in range(REACH)]

    for copy in loads[5:]:
        copy.wait()
    lens, slots = places_of(me)
    _, passing = places_of(lax.rem(me + groups - 2, groups))

    spots = lax.broadcasted_iota(jnp.int32, (piece, part), 1)

    def masked(ref, rows, slot):
        index, length, _ = slot
        block = ref[index, rows, :]
        return jnp.where(spots < length, block, jnp.zeros_like(block))

    n_copies = [
        remote(
            near.at[:, latent(i)], ac.at[pl.ds(0, CAPACITY), latent(i)],
            n_send.at[i], n_recv.at[i], on_group(1 - 2 * core),
        )
        for i in range(PIECES)
    ]
    loads[0].wait()

    @pl.when(core == 0)
    def _():
        for i in range(PIECES):
            for r in range(CAPACITY):
                near[r, latent(i), :] = masked(pctv, latent(i), slots[0][r])
            n_copies[i].start()

    far_slots = pl.ds((REACH - 1) * CAPACITY, CAPACITY)
    v_copies = [
        remote(
            given.at[:, latent(i)], via.at[:, latent(i)],
            v_send.at[i], v_recv.at[i], on_group(mid + 4),
        )
        for i in range(PIECES)
    ]
    b_copies = [
        remote(
            via.at[:, latent(i)], ac.at[far_slots, latent(i)],
            b_send.at[i], p_recv.at[i, REACH - 1], on_group(-mid),
        )
        for i in range(PIECES)
    ]

    @pl.when(giver)
    def _():
        for i in range(PIECES):
            for r in range(CAPACITY):
                given[r, latent(i), :] = masked(pctv, latent(i), slots[REACH - 1][r])
            v_copies[i].start()

    p_copies, keeps = [], []
    for i in range(PIECES):
        for d in range(1, REACH):
            src, dst = picked.at[d - 1, :, latent(i)], ac.at[pl.ds(d * CAPACITY, CAPACITY), latent(i)]
            if d == 1:
                keeps.append(pltpu.make_async_copy(src, dst, keep_sem.at[i]))
            else:
                p_copies.append(remote(src, dst, p_send.at[i, d], p_recv.at[i, d], on_group(d - 1)))

    def pass_on(i):
        w_copies[i].wait_recv()
        for d in range(REACH - 1, 0, -1):
            for r in range(CAPACITY):
                picked[d - 1, r, latent(i), :] = masked(wholes[i], slice(None), passing[d][r])
            if d == 1:
                keeps[i].start()
            else:
                copy = p_copies[i * (REACH - 2) + d - 2]
                if d == REACH - 1:
                    pl.when(jnp.logical_not(spared))(copy.start)
                else:
                    copy.start()

        @pl.when(core == 1)
        def _():
            for r in range(CAPACITY):
                near[r, latent(i), :] = masked(wholes[i], slice(None), passing[0][r])
            n_copies[i].start()

    def pass_when(*pieces, where):
        for i in pieces:
            pl.when(where)(functools.partial(pass_on, i))

    loads[4].wait()
    newkf[...] = jnp.zeros_like(newkf)
    for u in range(steps):
        step_rows = slv[u].astype(jnp.float32)
        for s in range(seqs):
            newkf[pl.ds(s * NEW_ROWS + u, 1), :] = step_rows[s:s + 1, :]
    newk[...] = newkf[...].astype(jnp.bfloat16)
    loads[2].wait()
    loads[3].wait()

    def resident(s):
        count = steps * heads
        query = rqv[:, s].reshape(count, width)
        fresh = newk.shape[0]
        old = matmul(query, rctv[s], NN) * SCALE
        new = matmul(query, newk[...], NT) * SCALE
        old_live = lax.broadcasted_iota(jnp.int32, (count, res_len), 1) < rlen[0, s]
        step = lax.broadcasted_iota(jnp.int32, (count, fresh), 0) // heads
        token = lax.broadcasted_iota(jnp.int32, (count, fresh), 1) - s * NEW_ROWS
        new_live = jnp.logical_and(token >= 0, token <= step)
        old = jnp.where(old_live, old, LOW)
        new = jnp.where(new_live, new, LOW)
        top = jnp.maximum(jnp.max(old, 1, keepdims=True), jnp.max(new, 1, keepdims=True))
        old = jnp.where(old_live, jnp.exp(old - top), 0.0)
        new = jnp.where(new_live, jnp.exp(new - top), 0.0)
        total = jnp.sum(old, 1, keepdims=True) + jnp.sum(new, 1, keepdims=True)
        mixed = matmul(old.astype(jnp.bfloat16), rctv[s, :LATENT_RANK, :], NT)
        mixed = mixed + matmul(new.astype(jnp.bfloat16), newk[:, :LATENT_RANK], NN)
        rov[:, s] = (mixed / total).astype(jnp.bfloat16).reshape(steps, heads, LATENT_RANK)

    for h in range(HALVES):
        q_copies[1, 0, h].wait_recv()
        for k in range(1, line):
            q_copies[1, k, h].start()

    for s in range(seqs // 2):
        resident(s)

    side = line * heads
    column = lax.broadcasted_iota(jnp.int32, (side, 128), 1)
    position = lax.broadcasted_iota(jnp.int32, (side, part), 1)
    o_copies = {0: [], 1: []}

    def send_back(copies):
        for copy in copies:
            copy.start()
        return copies

    def attend(j, chosen, stats):
        for p in chosen:
            query = qall[pl.ds(j * line, line), p].reshape(side, width)
            live = position < lens[p]
            scores = jnp.where(live, matmul(query, pctv[p], NN) * SCALE, LOW)
            top = jnp.max(scores, 1, keepdims=True)
            weights = jnp.where(live, jnp.exp(scores - top), 0.0)
            total = jnp.sum(weights, 1, keepdims=True)
            mixed = matmul(weights.astype(jnp.bfloat16), pctv[p, :LATENT_RANK, :], NT)
            obuf[pl.ds(j * line, line), p] = mixed.astype(jnp.bfloat16).reshape(line, heads, LATENT_RANK)
            stats = jnp.where(column == 2 * p, top, stats)
            stats = jnp.where(column == 2 * p + 1, total, stats)
        held, h = pl.ds(chosen[0], len(chosen)), chosen[0] // half
        o_copies[j] += send_back([
            remote(
                obuf.at[slot, held], rbuf.at[slot, held], o_send.at[slot, h], o_recv.at[slot, h],
                on_lane(0, (j + 1) * line - slot),
            )
            for slot in range(j * line + 1, (j + 1) * line)
        ])
        return stats

    def send_stats(j, stats):
        stat[pl.ds(j * line, line)] = stats.reshape(line, heads, 128)
        o_copies[j] += send_back([
            remote(
                stat.at[slot], rstat.at[slot], s_send.at[slot], s_recv.at[slot],
                on_lane(0, (j + 1) * line - slot),
            )
            for slot in range(j * line + 1, (j + 1) * line)
        ])

    def merged(p, parts):
        tops = [where[:, 2 * p:2 * p + 1] for where, _ in parts]
        sums = [where[:, 2 * p + 1:2 * p + 2] for where, _ in parts]
        top = functools.reduce(jnp.maximum, tops)
        total = jnp.zeros_like(top)
        mixed = jnp.zeros((heads, LATENT_RANK), jnp.float32)
        for own_top, own_sum, (_, values) in zip(tops, sums, parts):
            factor = jnp.exp(own_top - top)
            total = total + factor * own_sum
            mixed = mixed + factor * values[p].astype(jnp.float32)
        return top, total, mixed

    def parts_of(j):
        slots_of = [j * line + k for k in range(line)]
        return [
            ((stat if k == 0 else rstat).at[slot], (obuf if k == 0 else rbuf).at[slot])
            for k, slot in enumerate(slots_of)
        ]

    rest = jnp.logical_not(first)
    pass_when(0, where=rest)
    loads[1].wait()
    blank = jnp.zeros((side, 128), jnp.float32)
    for k in range(1, line):
        for h in range(HALVES):
            q_copies[0, k, h].wait_recv()
    send_stats(0, attend(0, range(prompts), blank))
    stats = blank
    for h in range(HALVES):
        for k in range(1, line):
            q_copies[1, k, h].wait_recv()
        stats = attend(1, range(h * half, (h + 1) * half), stats)
    send_stats(1, stats)

    @pl.when(bearer)
    def _():
        for there, on in zip(v_copies, b_copies):
            there.wait_recv()
            on.start()

    pass_when(1, 2, where=rest)
    for copy in o_copies[1]:
        copy.wait_recv()
    crossing = jnp.zeros((heads, 128), jnp.float32)
    lanes_of = lax.broadcasted_iota(jnp.int32, (heads, 128), 1)
    for p in range(prompts):
        top, total, mixed = merged(p, parts_of(1))
        xbuf[p] = mixed.astype(jnp.bfloat16)
        crossing = jnp.where(lanes_of == 2 * p, top, crossing)
        crossing = jnp.where(lanes_of == 2 * p + 1, total, crossing)
    xstat[...] = crossing
    crossings = ((xbuf, xrec, hop), (xstat, xrstat, hopstat))
    x_copies, out_copies, back_copies = [], [], []
    for i, (src, dst, via) in enumerate(crossings):
        x_copies.append(remote(src, dst, x_send.at[i], x_recv.at[i], on_lane(1, 0)))
        out_copies.append(remote(src, via, x_send.at[i], h_recv.at[i], beside(2)))
        back_copies.append(remote(via, dst, h_send.at[i], x_recv.at[i], on_group(-2)))

    @pl.when(first)
    def _():
        for copy in out_copies:
            copy.start()

    @pl.when(jnp.logical_not(first))
    def _():
        for copy in x_copies:
            copy.start()

    for s in range(seqs // 2, seqs):
        resident(s)
    pass_when(*range(PIECES), where=first)
    done = pltpu.make_async_copy(rov, ro, out_sem)
    done.start()

    for copy in o_copies[0]:
        copy.wait_recv()
    kept = jnp.zeros((heads, 128), jnp.float32)
    for p in range(prompts):
        top, total, mixed = merged(p, parts_of(0))
        mbuf[p] = mixed
        kept = jnp.where(lanes_of == 2 * p, top, kept)
        kept = jnp.where(lanes_of == 2 * p + 1, total, kept)
    mstat[...] = kept
    for copy in x_copies:
        copy.wait_recv()
    for p in range(prompts):
        _, total, mixed = merged(p, [(mstat, mbuf), (xrstat, xrec)])
        frows[p] = (mixed / jnp.maximum(total, 1.0)).astype(jnp.bfloat16)

    spread = lax.broadcasted_iota(jnp.int32, (heads, LATENT_RANK), 0)
    f_copies = []
    for d in range(REACH - 1, -1, -1):
        for r in range(CAPACITY):
            index, _, filled = slots[d][r]
            block = frows[index]
            fsend[d, r] = jnp.where(spread < filled * heads, block, jnp.zeros_like(block))
        copy = remote(
            fsend.at[d], fo.at[pl.ds(d * CAPACITY, CAPACITY)], f_send.at[d], f_recv.at[d], on_group(d + 1)
        )
        copy.start()
        f_copies.append(copy)

    @pl.when(second)
    def _():
        for out, back in zip(out_copies, back_copies):
            out.wait_recv()
            back.start()

    pass_when(3, where=rest)

    @pl.when(second)
    def _():
        for back in back_copies:
            back.wait_send()

    for copy in [done] + keeps:
        copy.wait()
    for copies in (q_copies.values(), o_copies[0], o_copies[1], x_copies, w_copies):
        for copy in copies:
            copy.wait_send()
    for copies in (n_copies, p_copies, f_copies):
        for copy in copies:
            copy.wait_recv()
    for copy in n_copies + f_copies:
        copy.wait_send()
    for i, copy in enumerate(p_copies):
        if i % (REACH - 2) == REACH - 3:
            pl.when(jnp.logical_not(spared))(copy.wait_send)
        else:
            copy.wait_send()
    for i in range(PIECES):
        pl.when(giver)(v_copies[i].wait_send)
        pl.when(bearer)(b_copies[i].wait_send)


def call(mesh_shape, plen, roff, rlen, sl, rct, rq, pct, pq):
    groups, lanes = mesh_shape
    prompts, width, part = pct.shape
    steps, seqs, heads, _ = rq.shape
    slots = REACH * CAPACITY
    bf, f32 = jnp.bfloat16, jnp.float32
    dma = pltpu.SemaphoreType.DMA
    anywhere = pl.BlockSpec(memory_space=pltpu.HBM)
    plen, roff, rlen, sl, rct, rq, pct, pq = [
        pltpu.with_memory_space_constraint(x, pltpu.HBM) for x in (plen, roff, rlen, sl, rct, rq, pct, pq)
    ]
    return pl.pallas_call(
        functools.partial(kernel, groups, lanes),
        out_shape=(
            jax.ShapeDtypeStruct((steps, seqs, heads, LATENT_RANK), bf),
            jax.ShapeDtypeStruct((slots, heads, LATENT_RANK), bf),
            jax.ShapeDtypeStruct((slots, width, part), bf),
        ),
        in_specs=[anywhere] * 8,
        out_specs=(pl.BlockSpec(memory_space=pl.ANY),) * 3,
        scratch_shapes=[
            pltpu.SMEM(plen.shape, jnp.int32),
            pltpu.SMEM(roff.shape, jnp.int32),
            pltpu.SMEM(rlen.shape, jnp.int32),
            pltpu.VMEM(rct.shape, bf),
            pltpu.VMEM(rq.shape, bf),
            pltpu.VMEM(pct.shape, bf),
            pltpu.VMEM(sl.shape, bf),
            pltpu.VMEM((lanes,) + pq.shape, bf),
            pltpu.VMEM((128, width), bf),
            pltpu.VMEM((128, width), f32),
            pltpu.VMEM((lanes, prompts, heads, LATENT_RANK), bf),
            pltpu.VMEM((lanes, prompts, heads, LATENT_RANK), bf),
            pltpu.VMEM((lanes, heads, 128), f32),
            pltpu.VMEM((lanes, heads, 128), f32),
            pltpu.VMEM((prompts, heads, LATENT_RANK), bf),
            pltpu.VMEM((prompts, heads, LATENT_RANK), bf),
            pltpu.VMEM((heads, 128), f32),
            pltpu.VMEM((heads, 128), f32),
            pltpu.VMEM((prompts, heads, LATENT_RANK), f32),
            pltpu.VMEM((heads, 128), f32),
            pltpu.VMEM((prompts, heads, LATENT_RANK), bf),
            pltpu.VMEM((heads, 128), f32),
            pltpu.VMEM((CAPACITY, width, part), bf),
            pltpu.VMEM((CAPACITY, width, part), bf),
            pltpu.VMEM((CAPACITY, width, part), bf),
            pltpu.VMEM((REACH - 1, CAPACITY, width, part), bf),
            pltpu.VMEM((prompts, heads, LATENT_RANK), bf),
            pltpu.VMEM((REACH, CAPACITY, heads, LATENT_RANK), bf),
            pltpu.VMEM((steps, seqs, heads, LATENT_RANK), bf),
            dma((8,)),
            dma,
            dma((lanes, HALVES)), dma((lanes, HALVES)),
            dma((lanes, HALVES)), dma((lanes, HALVES)),
            dma((lanes,)), dma((lanes,)),
            dma((2,)), dma((2,)),
            dma((2,)), dma((2,)),
            dma((PIECES,)), dma((PIECES,)),
            dma((PIECES,)), dma((PIECES,)),
            dma((PIECES, REACH)), dma((PIECES, REACH)),
            dma((PIECES,)),
            dma((REACH,)), dma((REACH,)),
            dma((PIECES,)), dma((PIECES,)), dma((PIECES,)),
        ] + [pltpu.VMEM((prompts, width // PIECES, part), bf)] * PIECES,
        compiler_params=pltpu.CompilerParams(
            collective_id=0, has_side_effects=True, vmem_limit_bytes=40 * 1024 * 1024
        ),
        name="decode_and_migrate",
    )(plen, roff, rlen, sl, rct, rq, pct, pq)


def writer(*refs):
    count = len(refs) // 2
    sems = refs[-1]
    copies = [pltpu.make_async_copy(refs[i], refs[count + i], sems.at[i]) for i in range(count)]
    for copy in copies:
        copy.start()
    for copy in copies:
        copy.wait()


def write_out(*arrays):
    arrays = [pltpu.with_memory_space_constraint(x, pltpu.VMEM) for x in arrays]
    return pl.pallas_call(
        writer,
        out_shape=tuple(jax.ShapeDtypeStruct(x.shape, x.dtype) for x in arrays),
        in_specs=[pl.BlockSpec(memory_space=pltpu.VMEM)] * len(arrays),
        out_specs=(pl.BlockSpec(memory_space=pltpu.HBM),) * len(arrays),
        scratch_shapes=[pltpu.SemaphoreType.DMA((len(arrays),))],
        name="write_out",
    )(*arrays)


def solution(mesh):
    mesh_shape = (mesh.shape["grp"], mesh.shape["head"])

    def body(
        resident_latent_cache, resident_len, resident_query, step_latent,
        prompt_cache, prompt_query, prompt_len, route_offset,
    ):
        ro, fo, ac = write_out(*call(
            mesh_shape,
            prompt_len.T,
            route_offset[:, :, 0].T,
            resident_len,
            step_latent,
            jnp.swapaxes(resident_latent_cache, 1, 2),
            resident_query,
            jnp.swapaxes(prompt_cache, 1, 2),
            prompt_query,
        ))
        return ro, fo[None], jnp.swapaxes(ac, 1, 2)[None]

    in_specs = (
        P("grp", None, None),
        P("grp", None),
        P(None, "grp", "head", None),
        P(None, "grp", None),
        P("grp", "head", None),
        P("grp", "head", None),
        P(),
        P(),
    )
    out_specs = (
        P(None, "grp", "head", None),
        P("grp", None, "head", None),
        P("grp", None, "head", None),
    )
    return jax.shard_map(body, mesh=mesh, in_specs=in_specs, out_specs=out_specs, check_vma=False)
```

profile of v0, /device:TPU:1, one launch (start us, length us, event | category | flops | bytes accessed | tf_op | source)
XLA Modules:
  0.0 42.1 jit_solution(8049382283450917104)
XLA Ops:
  0.6 40.3 %decode_and_migrate.1 = (bf16[3,4,16,512]{3,2,1,0:T(8,128)(2,1)S(1)}, bf16[8,16,512]{2,1,0:T(8,128)(2,1)S(1)}, bf16[8,576,128]{2,1,0:T(8,128)(2,1)S(1)}) custom-call(s32[4,64]{1,0:T(4,128)} %bitcast.12, s32[4,64]{1,0:T(4,128)} %bitcast.13, s32[1,4]{1,0:T(1,128)} %rlen_hbm.1, bf16[3,4,576]{2,1,0:T(4,128)(2,1)} %sl.1, bf16[4,576,256]{2,1,0:T(8,128)(2,1)} %bitcast.10, ...), custom_call_target="tpu_custom_call" | custom-call | tf_op jit(solution)/shard_map/decode_and_migrate/pallas_call | solution.py:457
  40.9 1.1 %write_out.1 = (bf16[3,4,16,512]{3,2,1,0:T(8,128)(2,1)}, bf16[8,16,512]{2,1,0:T(8,128)(2,1)}, bf16[8,576,128]{2,1,0:T(8,128)(2,1)}) custom-call(bf16[3,4,16,512]{3,2,1,0:T(8,128)(2,1)S(1)} %get-tuple-element.9.refs_0_, bf16[8,16,512]{2,1,0:T(8,128)(2,1)S(1)} %get-tuple-element.10.refs_1_, bf16[8,576,128]{2,1,0:T(8,128)(2,1)S(1)} %get-tuple-element.11.refs_2_), custom_call_target="tpu_custom_call" | custom-call | tf_op jit(solution)/shard_map/write_out/pallas_call | solution.py:529
where the time goes:
time: 42.4 us; the launch traced here: 42.1 us
  Pallas kernels  41.4 us (98%)
  between operations  0.64 us (2%)
    pallas_call x1, Pallas kernels, call(): pl.pallas_call(functools.partial(kernel, groups, lanes), out_shape=(jax.S...  40.3 us
    pallas_call x1, Pallas kernels, write_out(): pl.pallas_call(writer, out_shape=tuple((jax.ShapeDtypeStruct(x.shape, x.d...  1.15 us

commit v1 on v0

--- a/solution.py
+++ b/solution.py
@@ -32,7 +32,7 @@
     plen_hbm, roff_hbm, rlen_hbm, sl, rct, rq, pct, pq,
     ro, fo, ac,
     plen, roff, rlen,
-    rctv, rqv, pctv, slv, qall, newk, newkf, obuf, rbuf, stat, rstat, xbuf, xrec, xstat, xrstat, mbuf, mstat, hop, hopstat, given, via, near, picked, frows, fsend, rov,
+    rctv, rqv, pctv, slv, pqv, qall, ktail, newk, newkf, obuf, rbuf, stat, rstat, xbuf, xrec, xstat, xrstat, mbuf, mstat, hop, hopstat, given, via, near, picked, frows, fsend, rov,
     load_sem, out_sem, q_send, q_recv, o_send, o_recv, s_send, s_recv, x_send, x_recv, h_send, h_recv,
     w_send, w_recv, n_send, n_recv, p_send, p_recv, keep_sem, f_send, f_recv, v_send, v_recv, b_send,
     *wholes,
@@ -84,12 +84,21 @@
 
     loads = [
         pltpu.make_async_copy(src, dst, load_sem.at[i])
-        for i, (src, dst) in enumerate(((pct, pctv), (pq, qall.at[0]), (rct, rctv), (rq, rqv), (sl, slv),
+        for i, (src, dst) in enumerate(((pct, pctv), (pq, pqv), (rct, rctv), (rq, rqv), (sl, slv),
                                     (plen_hbm, plen), (roff_hbm, roff), (rlen_hbm, rlen)))
     ]
     for copy in loads:
         copy.start()
 
+    half = prompts // HALVES
+    tail = width - LATENT_RANK
+    loads[1].wait()
+    for h in range(HALVES):
+        for i in range(half):
+            qall[0, h, :, pl.ds(i * LATENT_RANK, LATENT_RANK)] = pqv[h * half + i, :, :LATENT_RANK]
+        tails = [pqv[h * half + i, :, LATENT_RANK:] for i in range(half)]
+        qall[0, h, :, pl.ds(half * LATENT_RANK, half * tail)] = jnp.concatenate(tails, axis=1)
+
     extra = core + jnp.where(jnp.logical_or(first, second), 1, 0)
     extra = extra + jnp.where(jnp.logical_or(giver, bearer), 1, 0)
     pl.semaphore_wait(barrier, len(direct) + REACH + extra)
@@ -99,12 +108,9 @@
             src_ref=src, dst_ref=dst, send_sem=send, recv_sem=recv, device_id=to, device_id_type=MESH
         )
 
-    half = prompts // HALVES
-
     def query_copy(j, k, h):
-        slot, held = j * line + k, pl.ds(h * half, half)
-        source = qall.at[j * line, held] if j and k else pq.at[held]
-        return remote(source, qall.at[slot, held], q_send.at[slot, h], q_recv.at[slot, h], on_lane(0 if k else j, k))
+        slot, source = j * line + k, qall.at[j * line if j and k else 0, h]
+        return remote(source, qall.at[slot, h], q_send.at[slot, h], q_recv.at[slot, h], on_lane(0 if k else j, k))
 
     q_copies = {(j, k, h): query_copy(j, k, h) for j, k in others for h in range(HALVES)}
     for h in range(HALVES):
@@ -227,6 +233,10 @@
     def pass_when(*pieces, where):
         for i in pieces:
             pl.when(where)(functools.partial(pass_on, i))
+
+    ktail[...] = jnp.zeros_like(ktail)
+    for p in range(prompts):
+        ktail[p, pl.ds(p % half * tail, tail), :] = pctv[p, LATENT_RANK:, :]
 
     loads[4].wait()
     newkf[...] = jnp.zeros_like(newkf)
@@ -278,9 +288,13 @@
 
     def attend(j, chosen, stats):
         for p in chosen:
-            query = qall[pl.ds(j * line, line), p].reshape(side, width)
+            h, place = p // half, p % half
+            query = qall[pl.ds(j * line, line), h, :, pl.ds(place * LATENT_RANK, LATENT_RANK)]
+            rest_of = qall[pl.ds(j * line, line), h, :, pl.ds(half * LATENT_RANK, half * tail)]
+            scores = matmul(query.reshape(side, LATENT_RANK), pctv[p, :LATENT_RANK, :], NN)
+            scores = scores + matmul(rest_of.reshape(side, half * tail), ktail[p], NN)
             live = position < lens[p]
-            scores = jnp.where(live, matmul(query, pctv[p], NN) * SCALE, LOW)
+            scores = jnp.where(live, scores * SCALE, LOW)
             top = jnp.max(scores, 1, keepdims=True)
             weights = jnp.where(live, jnp.exp(scores - top), 0.0)
             total = jnp.sum(weights, 1, keepdims=True)
@@ -329,7 +343,6 @@
 
     rest = jnp.logical_not(first)
     pass_when(0, where=rest)
-    loads[1].wait()
     blank = jnp.zeros((side, 128), jnp.float32)
     for k in range(1, line):
         for h in range(HALVES):
@@ -471,7 +484,9 @@
             pltpu.VMEM(rq.shape, bf),
             pltpu.VMEM(pct.shape, bf),
             pltpu.VMEM(sl.shape, bf),
-            pltpu.VMEM((lanes,) + pq.shape, bf),
+            pltpu.VMEM(pq.shape, bf),
+            pltpu.VMEM((lanes, HALVES, heads, prompts // HALVES * width), bf),
+            pltpu.VMEM((prompts, prompts // HALVES * (width - LATENT_RANK), part), bf),
             pltpu.VMEM((128, width), bf),
             pltpu.VMEM((128, width), f32),
             pltpu.VMEM((lanes, prompts, heads, LATENT_RANK), bf),

time: 42.4 us -> 42.1 us (level)
  no operation moved by 1% of the time
where the time goes in v1:
time: 42.1 us; the launch traced here: 41.8 us
  Pallas kernels  41.1 us (98%)
  between operations  0.64 us (2%)
    pallas_call x1, Pallas kernels, call(): pl.pallas_call(functools.partial(kernel, groups, lanes), out_shape=(jax.S...  40 us
    pallas_call x1, Pallas kernels, write_out(): pl.pallas_call(writer, out_shape=tuple((jax.ShapeDtypeStruct(x.shape, x.d...  1.15 us

profile of v1, /device:TPU:1, one launch (start us, length us, event | category | flops | bytes accessed | tf_op | source)
XLA Modules:
  0.0 41.8 jit_solution(2438635381198423409)
XLA Ops:
  0.6 40.0 %decode_and_migrate.1 = (bf16[3,4,16,512]{3,2,1,0:T(8,128)(2,1)S(1)}, bf16[8,16,512]{2,1,0:T(8,128)(2,1)S(1)}, bf16[8,576,128]{2,1,0:T(8,128)(2,1)S(1)}) custom-call(s32[4,64]{1,0:T(4,128)} %bitcast.12, s32[4,64]{1,0:T(4,128)} %bitcast.13, s32[1,4]{1,0:T(1,128)} %rlen_hbm.1, bf16[3,4,576]{2,1,0:T(4,128)(2,1)} %sl.1, bf16[4,576,256]{2,1,0:T(8,128)(2,1)} %bitcast.10, ...), custom_call_target="tpu_custom_call" | custom-call | tf_op jit(solution)/shard_map/decode_and_migrate/pallas_call | solution.py:470
  40.6 1.1 %write_out.1 = (bf16[3,4,16,512]{3,2,1,0:T(8,128)(2,1)}, bf16[8,16,512]{2,1,0:T(8,128)(2,1)}, bf16[8,576,128]{2,1,0:T(8,128)(2,1)}) custom-call(bf16[3,4,16,512]{3,2,1,0:T(8,128)(2,1)S(1)} %get-tuple-element.9.refs_0_, bf16[8,16,512]{2,1,0:T(8,128)(2,1)S(1)} %get-tuple-element.10.refs_1_, bf16[8,576,128]{2,1,0:T(8,128)(2,1)S(1)} %get-tuple-element.11.refs_2_), custom_call_target="tpu_custom_call" | custom-call | tf_op jit(solution)/shard_map/write_out/pallas_call | solution.py:544
